TPU v7x, 32 devices: a whole 2x2x4 slice. The times are simulated.
32 devices in a mesh: seq: 8 (over z, y), ch: 4 (over x, core).
Axes of the slice: x: 2, y: 2, z: 4, core: 2. Of those that a mesh axis runs over, the one named last changes fastest.
Arguments:
- query_rows: bfloat16 [2048, 4096], P(('seq', 'ch')), may hold values from -6 to 6
- key_rows: bfloat16 [2048, 4096], P(('seq', 'ch')), may hold values from -6 to 6
- value_rows: bfloat16 [2048, 4096], P(('seq', 'ch')), may hold values from -6 to 6
- filter_taps: float32 [2048, 4096], P(('seq', 'ch')), may hold values from -1.1 to 1.1
- skip_gain: float32 [4096], replicated, may hold values from 0.5 to 1.5
Outputs:
- gated_output: bfloat16 [2048, 4096], P(('seq', 'ch'))
All inputs are finite; a program needn't handle non-finite values.
Results may differ from a plain program's by a relative error of at most 0.0014.
Values sent between devices are 32-bit elements; how exact they have to be, the bound alone decides.
A program may use at most 128 MiB of HBM per device.

v0:
```python
import math
import jax
import jax.numpy as jnp
from jax import lax
from jax.sharding import PartitionSpec as P

highest = lax.Precision.HIGHEST


def angles(product_ids, modulus):
    return 2.0 * math.pi / modulus * (product_ids % modulus).astype(jnp.float32)


def contract(pattern, weights, operand):
    return jnp.einsum(
        pattern, weights, operand, precision=highest, preferred_element_type=jnp.float32
    )


def shards(query_rows, key_rows, value_rows, filter_taps, skip_gain):
    seq_count = lax.axis_size("seq")
    group_count = lax.axis_size("ch")
    position = lax.axis_index("seq")
    row_count, full_width = key_rows.shape
    per_peer = row_count // seq_count
    columns = full_width // group_count
    local_rows = group_count * per_peer
    tokens = row_count * group_count
    slot_count = 2 * seq_count
    length = 2 * tokens * seq_count
    signal = key_rows.astype(jnp.float32) * value_rows.astype(jnp.float32)
    layout = (1, seq_count, 1, per_peer, full_width)
    moved_signal, moved_filter = (
        lax.all_to_all(
            lax.all_to_all(signal.reshape(layout), "seq", split_axis=1, concat_axis=0, tiled=True),
            "ch",
            split_axis=4,
            concat_axis=2,
            tiled=True,
        ),
        lax.all_to_all(
            lax.all_to_all(
                filter_taps.reshape(layout), "seq", split_axis=1, concat_axis=0, tiled=True
            ),
            "ch",
            split_axis=4,
            concat_axis=2,
            tiled=True,
        ),
    )
    moved_signal = moved_signal.reshape(seq_count, local_rows, columns)
    moved_filter = moved_filter.reshape(seq_count, local_rows, columns)
    slot_ids = jnp.arange(slot_count, dtype=jnp.int32)
    owners = slot_ids // 2
    freq_slot = jnp.where(
        slot_ids % 2 == 0, owners, jnp.where(owners == 0, seq_count, slot_count - owners)
    )
    blocks = jnp.arange(seq_count, dtype=jnp.int32)
    block_phase = angles(freq_slot[:, None] * blocks[None, :], slot_count)
    block_cos = jnp.cos(block_phase)
    block_sin = jnp.sin(block_phase)
    local_ids = jnp.arange(local_rows, dtype=jnp.int32)
    local_time = local_ids // per_peer * row_count + position * per_peer + local_ids % per_peer
    twist_angle = -angles(freq_slot[:, None] * local_time[None, :], length)
    twist_cos = jnp.cos(twist_angle)[:, :, None]
    twist_sin = jnp.sin(twist_angle)[:, :, None]

    def forward_blocks(real_part):
        out_real = contract("jd,dmc->jmc", block_cos, real_part)
        out_imag = -contract("jd,dmc->jmc", block_sin, real_part)
        return jnp.stack(
            [
                out_real * twist_cos - out_imag * twist_sin,
                out_real * twist_sin + out_imag * twist_cos,
            ]
        )

    all_ids = jnp.arange(tokens, dtype=jnp.int32)
    peer_id = all_ids // local_rows
    within = all_ids % local_rows
    all_time = within // per_peer * row_count + peer_id * per_peer + within % per_peer
    inner_phase = angles(all_ids[:, None] * all_time[None, :], tokens)
    inner_cos = jnp.cos(inner_phase)
    inner_sin = jnp.sin(inner_phase)

    def forward_inner(spectrum):
        real_part = spectrum[0]
        imag_part = spectrum[1]
        out_real = contract("qp,jpc->jqc", inner_cos, real_part) + contract(
            "qp,jpc->jqc", inner_sin, imag_part
        )
        out_imag = contract("qp,jpc->jqc", inner_cos, imag_part) - contract(
            "qp,jpc->jqc", inner_sin, real_part
        )
        return (out_real, out_imag)

    signal_spectrum, filter_spectrum = (
        lax.all_to_all(
            forward_blocks(moved_signal), "seq", split_axis=1, concat_axis=2, tiled=True
        ),
        lax.all_to_all(
            forward_blocks(moved_filter), "seq", split_axis=1, concat_axis=2, tiled=True
        ),
    )
    signal_real, signal_imag = forward_inner(signal_spectrum)
    filter_real, filter_imag = forward_inner(filter_spectrum)
    product_real = signal_real * filter_real - signal_imag * filter_imag
    product_imag = signal_real * filter_imag + signal_imag * filter_real
    back_real = contract("qp,jqc->jpc", inner_cos, product_real) - contract(
        "qp,jqc->jpc", inner_sin, product_imag
    )
    back_imag = contract("qp,jqc->jpc", inner_cos, product_imag) + contract(
        "qp,jqc->jpc", inner_sin, product_real
    )
    my_slots = jnp.stack([position, jnp.where(position == 0, seq_count, slot_count - position)])
    back_phase = angles(my_slots[:, None] * all_time[None, :], length)[:, :, None]
    back_cos = jnp.cos(back_phase)
    back_sin = jnp.sin(back_phase)
    turned_real = back_real * back_cos - back_imag * back_sin
    turned_imag = back_real * back_sin + back_imag * back_cos
    inverse_scale = 1.0 / length
    gathered = lax.all_to_all(
        jnp.stack([turned_real, turned_imag]), "seq", split_axis=2, concat_axis=1, tiled=True
    )
    convolved = (
        contract("jd,jmc->dmc", block_cos, gathered[0])
        - contract("jd,jmc->dmc", block_sin, gathered[1])
    ) * inverse_scale
    returned = lax.all_to_all(
        lax.all_to_all(
            convolved.reshape(seq_count, 1, group_count, per_peer, columns),
            "seq",
            split_axis=0,
            concat_axis=1,
            tiled=True,
        ),
        "ch",
        split_axis=2,
        concat_axis=4,
        tiled=True,
    )
    convolved_rows = returned.reshape(row_count, full_width)
    gated = query_rows.astype(jnp.float32) * (convolved_rows + skip_gain[None, :] * signal)
    return gated.astype(jnp.bfloat16)


def solution(mesh):
    in_specs = (
        P(("seq", "ch"), None),
        P(("seq", "ch"), None),
        P(("seq", "ch"), None),
        P(("seq", "ch"), None),
        P(),
    )
    out_specs = P(("seq", "ch"), None)
    return jax.shard_map(shards, mesh=mesh, in_specs=in_specs, out_specs=out_specs, check_vma=False)
```

profile of v0, /device:TPU:0, one launch (start us, length us, event | category | flops | bytes accessed | tf_op | source)
XLA Modules:
  0.0 577.8 jit_solution(11160475574549039905)
XLA Ops:
  0.0 7.4 %all-to-all-start.3 = ((f32[1,8,1,8,4096]{4,3,2,0,1:T(8,128)}), f32[1,8,1,8,4096]{4,3,2,0,1:T(8,128)S(1)}, u32[]{:S(2)}, u32[]{:S(2)}) async-start(f32[1,8,1,8,4096]{4,3,2,0,1:T(8,128)} %bitcast.167), calls=%async_computation.3 | async-start | bytes 2097152 | tf_op jit(solution)/shard_map/all_to_all | solution.py:42
  7.4 1.1 fusion.15
  8.5 24.7 %all-to-all-done.3 = f32[1,8,1,8,4096]{4,3,2,0,1:T(8,128)S(1)} async-done(((f32[1,8,1,8,4096]{4,3,2,0,1:T(8,128)}), f32[1,8,1,8,4096]{4,3,2,0,1:T(8,128)S(1)}, u32[]{:S(2)}, u32[]{:S(2)}) %all-to-all-start.3) | async-done | bytes 1048608 | tf_op jit(solution)/shard_map/all_to_all | solution.py:42
  33.2 3.6 all-to-all-start
  36.8 8.7 %copy.61 = f32[8,1,1,8,4096]{3,0,2,1,4:T(8,128)} copy(f32[8,1,1,8,4096]{4,3,0,2,1:T(8,128)S(1)} %bitcast.159) | data formatting | bytes 2097152 | tf_op jit(solution)/shard_map/all_to_all | solution.py:42
  45.5 11.9 %reshape.292 = f32[4,1,65536]{2,1,0:T(1,128)} reshape(f32[4096,1,1,8,8]{4,3,2,1,0:T(8,128)} %bitcast.139) | data formatting | bytes 2097152
  57.4 5.3 all-to-all-done
  62.7 3.5 all-to-all-start.4
  66.3 8.7 %copy.52 = f32[8,1,1,8,4096]{3,0,2,1,4:T(8,128)} copy(f32[8,1,1,8,4096]{4,3,0,2,1:T(8,128)S(1)} %bitcast.158) | data formatting | bytes 2097152 | tf_op jit(solution)/shard_map/all_to_all | solution.py:35
  75.0 11.9 %reshape.290 = f32[4,1,65536]{2,1,0:T(1,128)} reshape(f32[4096,1,1,8,8]{4,3,2,1,0:T(8,128)} %bitcast.140) | data formatting | bytes 2097152
  86.9 4.7 all-to-all-start.1
  92.3 3.7 reduce
  96.0 14.8 %reshape.293 = f32[4096,1,1,8,8]{4,3,2,1,0:T(8,128)} reshape(f32[4,65536]{1,0:T(4,128)S(1)} %reduce) | data formatting | bytes 2097152
  110.8 10.0 %copy.90 = f32[8,1,1,8,4,1024]{5,4,3,0,2,1:T(4,128)S(1)} copy(f32[8,1,1,8,4,1024]{3,0,5,4,2,1:T(8,128)} %bitcast.141) | data formatting | bytes 2097152 | tf_op jit(solution)/shard_map/all_to_all | solution.py:41
  120.8 0.6 copy.63
  121.4 1.9 fusion.62
  123.3 3.2 fusion.68
  126.6 4.6 reduce.1
  131.2 15.0 %reshape.291 = f32[4096,1,1,8,8]{4,3,2,1,0:T(8,128)} reshape(f32[4,65536]{1,0:T(4,128)S(1)} %reduce.1) | data formatting | bytes 2097152
  146.2 9.8 %copy.89 = f32[8,1,1,8,4,1024]{5,4,3,0,2,1:T(4,128)S(1)} copy(f32[8,1,1,8,4,1024]{3,0,5,4,2,1:T(8,128)} %bitcast.142) | data formatting | bytes 2097152 | tf_op jit(solution)/shard_map/all_to_all | solution.py:34
  156.0 0.6 copy.54
  156.7 1.9 fusion.64
  158.6 4.8 subtract_bitcast_fusion.1
  164.0 4.4 copy.64
  168.4 4.7 all-to-all-start.5
  173.1 2.0 pad_maximum_fusion
  175.1 4.4 copy.55
  179.6 87.6 %all-to-all-done.5 = f32[2,16,32,1024]{3,2,0,1:T(8,128)} async-done(((f32[2,16,32,1024]{3,2,0,1:T(8,128)}), f32[2,16,32,1024]{3,2,0,1:T(8,128)}, u32[]{:S(2)}, u32[]{:S(2)}) %all-to-all-start.5) | async-done | bytes 4194336 | tf_op jit(solution)/shard_map/all_to_all | solution.py:101
  267.2 5.0 all-to-all-start.2
  272.4 2.5 copy.65
  274.9 0.6 fusion.169
  276.0 4.4 fusion.31
  280.5 5.8 %fusion.27 = f32[2,1024,256]{2,1,0:T(8,128)} fusion(f32[2,256,1024]{2,1,0:T(8,128)S(1)} %bitcast.145, s32[256]{0:T(256)S(1)} %fusion.88), kind=kOutput, calls=%fused_computation.45 | convolution fusion | flops 1611530240 | bytes 4195328 | tf_op jit(solution)/shard_map/qp,jpc->jqc/dot_general | solution.py:15
  286.3 6.0 %convolution_add_fusion = f32[2,1024,256]{2,1,0:T(8,128)} fusion(f32[2,1024,256]{2,1,0:T(8,128)S(1)} %fusion.31, f32[2,256,1024]{2,1,0:T(8,128)S(1)} %bitcast.146, s32[256]{0:T(256)S(1)} %fusion.88), kind=kOutput, calls=%fused_computation.23 | convolution fusion | flops 1612054528 | bytes 6292480 | tf_op jit(solution)/shard_map/qp,jpc->jqc/dot_general | solution.py:15
  292.3 72.9 %all-to-all-done.2 = f32[2,16,32,1024]{3,2,0,1:T(8,128)} async-done(((f32[2,16,32,1024]{3,2,0,1:T(8,128)}), f32[2,16,32,1024]{3,2,0,1:T(8,128)}, u32[]{:S(2)}, u32[]{:S(2)}) %all-to-all-start.2) | async-done | bytes 4194336 | tf_op jit(solution)/shard_map/all_to_all | solution.py:98
  365.1 2.5 copy.56
  367.6 0.6 fusion.170
  368.5 4.4 fusion.33
  373.1 4.5 fusion.29
  377.6 4.7 convolution_add_fusion.1
  382.4 4.3 convolution_subtract_fusion
  386.7 5.0 multiply_subtract_fusion
  391.7 2.8 fusion.2
  394.6 2.8 fusion
  397.4 2.8 fusion.8
  400.3 3.4 subtract_bitcast_fusion
  403.6 2.2 pad_maximum_fusion.2
  405.8 7.4 %copy.74 = f32[2,2,256,1024]{3,1,0,2:T(2,128)} copy(f32[2,2,256,1024]{2,3,1,0:T(8,128)} %pad_maximum_fusion.2) | data formatting | bytes 8388608 | tf_op jit(solution)/shard_map/stack | solution.py:123
  413.3 96.9 %all_to_all.126 = f32[2,2,256,1024]{3,1,0,2:T(2,128)S(1)} all-to-all(f32[2,2,256,1024]{3,1,0,2:T(2,128)} %copy.74), channel_id=1, replica_groups=mesh['seq'=8,'ch'=4] {'seq'}, dimensions={2} | all-to-all | bytes 8388608 | tf_op jit(solution)/shard_map/all_to_all | solution.py:122
  510.2 2.4 copy.75
  512.6 1.8 fusion.168
  514.4 1.6 copy.76
  516.0 2.4 squeeze.22
  518.5 2.9 fusion.66
  521.4 3.0 copy.77
  524.3 2.7 squeeze.23
  527.0 1.1 fusion.14
  528.2 0.6 copy.78
  528.8 28.9 %all_to_all.127 = f32[8,1,4,8,1024]{4,3,2,1,0:T(8,128)S(1)} all-to-all(f32[8,1,4,8,1024]{4,3,2,1,0:T(8,128)S(1)} %copy.78), channel_id=1, replica_groups=mesh['seq'=8,'ch'=4] {'seq'}, dimensions={0} | all-to-all | bytes 2097152 | tf_op jit(solution)/shard_map/all_to_all | solution.py:130
  557.7 0.6 copy.79
  558.3 16.9 %all_to_all.128 = f32[1,8,4,8,1024]{4,1,3,0,2:T(8,128)S(1)} all-to-all(f32[1,8,4,8,1024]{4,1,3,0,2:T(8,128)S(1)} %copy.79), channel_id=1, replica_groups=mesh['seq'=8,'ch'=4] {'ch'}, dimensions={2} | all-to-all | bytes 2097152 | tf_op jit(solution)/shard_map/all_to_all | solution.py:129
  575.2 0.7 copy.93
  575.9 0.6 copy.91
  576.5 1.1 multiply_convert_fusion
  (36 shorter events, 2.5 us)
Async XLA Ops:
  0.0 7.4 %copy-start.7 = (bf16[64,4096]{1,0:T(8,128)(2,1)S(1)}, bf16[64,4096]{1,0:T(8,128)(2,1)}, u32[]{:S(2)}) copy-start(bf16[64,4096]{1,0:T(8,128)(2,1)} %param.6) | copy-start | bytes 1572868
  0.0 7.4 %copy-start.5 = (bf16[64,4096]{1,0:T(8,128)(2,1)S(1)}, bf16[64,4096]{1,0:T(8,128)(2,1)}, u32[]{:S(2)}) copy-start(bf16[64,4096]{1,0:T(8,128)(2,1)} %param.7) | copy-start | bytes 1572868
  0.0 33.2 %all-to-all-start.3 = ((f32[1,8,1,8,4096]{4,3,2,0,1:T(8,128)}), f32[1,8,1,8,4096]{4,3,2,0,1:T(8,128)S(1)}, u32[]{:S(2)}, u32[]{:S(2)}) async-start(f32[1,8,1,8,4096]{4,3,2,0,1:T(8,128)} %bitcast.167), calls=%async_computation.3 | async-start | bytes 2097152 | tf_op jit(solution)/shard_map/all_to_all | solution.py:42
  33.2 29.5 %all-to-all-start = ((f32[1,8,1,8,4096]{4,3,2,0,1:T(8,128)}), f32[1,8,1,8,4096]{4,3,2,0,1:T(8,128)S(1)}, u32[]{:S(2)}, u32[]{:S(2)}) async-start(f32[1,8,1,8,4096]{4,3,2,0,1:T(8,128)} %fusion.15), calls=%async_computation | async-start | bytes 2097152 | tf_op jit(solution)/shard_map/all_to_all | solution.py:35
  62.7 24.2 %all-to-all-start.4 = ((f32[4,1,65536]{2,1,0:T(1,128)}), f32[4,1,65536]{2,1,0:T(1,128)S(1)}, u32[]{:S(2)}, u32[]{:S(2)}) async-start(f32[4,1,65536]{2,1,0:T(1,128)} %reshape.292), calls=%async_computation.4 | async-start | bytes 2097152 | tf_op jit(solution)/shard_map/all_to_all | solution.py:41
  86.9 39.6 %all-to-all-start.1 = ((f32[4,1,65536]{2,1,0:T(1,128)}), f32[4,1,65536]{2,1,0:T(1,128)}, u32[]{:S(2)}, u32[]{:S(2)}) async-start(f32[4,1,65536]{2,1,0:T(1,128)} %reshape.290), calls=%async_computation.1 | async-start | bytes 2097152 | tf_op jit(solution)/shard_map/all_to_all | solution.py:34
  156.6 1.9 copy-start
  168.4 4.7 copy-start.2
  168.4 98.8 %all-to-all-start.5 = ((f32[2,16,32,1024]{3,2,0,1:T(8,128)}), f32[2,16,32,1024]{3,2,0,1:T(8,128)}, u32[]{:S(2)}, u32[]{:S(2)}) async-start(f32[2,16,32,1024]{3,2,0,1:T(8,128)} %copy.64), calls=%async_computation.5 | async-start | bytes 8388608 | tf_op jit(solution)/shard_map/all_to_all | solution.py:101
  267.2 97.9 %all-to-all-start.2 = ((f32[2,16,32,1024]{3,2,0,1:T(8,128)}), f32[2,16,32,1024]{3,2,0,1:T(8,128)}, u32[]{:S(2)}, u32[]{:S(2)}) async-start(f32[2,16,32,1024]{3,2,0,1:T(8,128)} %copy.55), calls=%async_computation.2 | async-start | bytes 8388608 | tf_op jit(solution)/shard_map/all_to_all | solution.py:98
  377.6 4.7 copy-start.1
  382.4 4.3 copy-start.4
  518.5 2.9 copy-start.3
  575.2 1.3 copy-start.6
  575.2 1.3 copy-start.8
  575.2 1.4 copy-start.9
  575.2 1.4 copy-start.10
where the time goes:
time: 584 us; the launch traced here: 578 us
  waiting for transfers between devices  190 us (33%)
  blocking collectives  143 us (24%)
  local copies, waits for them, and re-layouts  133 us (23%)
  matrix products  66.9 us (11%)
  starting transfers between devices  28.9 us (5%)
  other arithmetic  15.6 us (3%)
    all_to_all x1, blocking collectives, shards(): lax.all_to_all(jnp.stack([turned_real, turned_imag]), 'seq', split_axis=2...  96.9 us
    all_to_all x1, waiting for transfers between devices, shards(): lax.all_to_all(forward_blocks(moved_filter), 'seq', split_axis=1, concat_...  87.6 us
    all_to_all x1, waiting for transfers between devices, shards(): lax.all_to_all(forward_blocks(moved_signal), 'seq', split_axis=1, concat_...  72.9 us
    dot_general x18, matrix products, contract(): jnp.einsum(pattern, weights, operand, precision=highest, preferred_elemen...  66.9 us
    unnamed x27, local copies, waits for them, and re-layouts  54.3 us
    all_to_all x1, blocking collectives, shards(): lax.all_to_all(convolved.reshape(seq_count, 1, group_count, per_peer, col...  28.9 us
    all_to_all x1, waiting for transfers between devices, shards(): lax.all_to_all(filter_taps.reshape(layout), 'seq', split_axis=1, concat_a...  24.7 us
    all_to_all x1, blocking collectives, shards(): lax.all_to_all(lax.all_to_all(convolved.reshape(seq_count, 1, group_count...  16.9 us
  transfers between devices with their start and end apart: 6, of which 4 were waited for; matrix products, arithmetic and copies ran while one was open for 18% of the time, Pallas kernels for 0%

commit v1 on v0

--- a/solution.py
+++ b/solution.py
@@ -38,14 +38,26 @@
             concat_axis=2,
             tiled=True,
         ),
-        lax.all_to_all(
+        jnp.concatenate(
             lax.all_to_all(
-                filter_taps.reshape(layout), "seq", split_axis=1, concat_axis=0, tiled=True
+                jnp.stack(
+                    jnp.split(
+                        lax.all_to_all(
+                            filter_taps.reshape(layout),
+                            "seq",
+                            split_axis=1,
+                            concat_axis=0,
+                            tiled=True,
+                        ),
+                        lax.axis_size("ch"),
+                        axis=4,
+                    )
+                ),
+                "ch",
+                0,
+                0,
             ),
-            "ch",
-            split_axis=4,
-            concat_axis=2,
-            tiled=True,
+            axis=2,
         ),
     )
     moved_signal = moved_signal.reshape(seq_count, local_rows, columns)

time: 584 us -> 561 us (0.961)
  local copies, waits for them, and re-layouts: 133 us -> 88.2 us
  waiting for transfers between devices: 190 us -> 217 us
    unnamed x27 -> x25, local copies, waits for them, and re-layouts: 54.3 us -> 27.6 us
    all_to_all x4 -> x0, local copies, waits for them, and re-layouts: 19.9 us -> none  [the longest x3 11.1 us: shards(): lax.all_to_all(lax.all_to_all(filter_taps.reshape(layout), 'seq', split_a...]
    all_to_all x1, waiting for transfers between devices: 5.3 us -> 24.2 us  [shards(): lax.all_to_all(signal.reshape(layout), 'seq', split_axis=1, concat_axis=0...]
    all_to_all x1, waiting for transfers between devices: 0.01 us -> 9.08 us  [shards(): lax.all_to_all(lax.all_to_all(signal.reshape(layout), 'seq', split_axis=1...]
  transfers between devices with their start and end apart: 6 -> 6, of which waited for: 4 -> 5; matrix products, arithmetic and copies ran while one was open for 18% -> 10% of each run, Pallas kernels for 0% -> 0%
where the time goes in v1:
time: 561 us; the launch traced here: 556 us
  waiting for transfers between devices  217 us (39%)
  blocking collectives  143 us (25%)
  local copies, waits for them, and re-layouts  88.2 us (16%)
  matrix products  67 us (12%)
  starting transfers between devices  28.7 us (5%)
  other arithmetic  12 us (2%)
    all_to_all x1, blocking collectives, shards(): lax.all_to_all(jnp.stack([turned_real, turned_imag]), 'seq', split_axis=2...  96.9 us
    all_to_all x1, waiting for transfers between devices, shards(): lax.all_to_all(forward_blocks(moved_filter), 'seq', split_axis=1, concat_...  86.8 us
    all_to_all x1, waiting for transfers between devices, shards(): lax.all_to_all(forward_blocks(moved_signal), 'seq', split_axis=1, concat_...  72 us
    dot_general x18, matrix products, contract(): jnp.einsum(pattern, weights, operand, precision=highest, preferred_elemen...  67 us
    all_to_all x1, blocking collectives, shards(): lax.all_to_all(convolved.reshape(seq_count, 1, group_count, per_peer, col...  28.9 us
    unnamed x25, local copies, waits for them, and re-layouts  27.6 us
    all_to_all x1, waiting for transfers between devices, shards(): lax.all_to_all(filter_taps.reshape(layout), 'seq', split_axis=1, concat_a...  24.7 us
    all_to_all x1, waiting for transfers between devices, shards(): lax.all_to_all(signal.reshape(layout), 'seq', split_axis=1, concat_axis=0...  24.2 us
  transfers between devices with their start and end apart: 6, of which 5 were waited for; matrix products, arithmetic and copies ran while one was open for 10% of the time, Pallas kernels for 0%

profile of v1, /device:TPU:0, one launch (start us, length us, event | category | flops | bytes accessed | tf_op | source)
XLA Modules:
  0.0 555.8 jit_solution(3673926719187434732)
XLA Ops:
  0.0 7.4 %all-to-all-start.3 = ((f32[1,8,1,8,4096]{4,3,2,0,1:T(8,128)}), f32[1,8,1,8,4096]{4,3,2,0,1:T(8,128)S(1)}, u32[]{:S(2)}, u32[]{:S(2)}) async-start(f32[1,8,1,8,4096]{4,3,2,0,1:T(8,128)} %bitcast.170), calls=%async_computation.3 | async-start | bytes 2097152 | tf_op jit(solution)/shard_map/all_to_all | solution.py:45
  7.4 1.1 fusion.15
  8.5 24.7 %all-to-all-done.3 = f32[1,8,1,8,4096]{4,3,2,0,1:T(8,128)S(1)} async-done(((f32[1,8,1,8,4096]{4,3,2,0,1:T(8,128)}), f32[1,8,1,8,4096]{4,3,2,0,1:T(8,128)S(1)}, u32[]{:S(2)}, u32[]{:S(2)}) %all-to-all-start.3) | async-done | bytes 1048608 | tf_op jit(solution)/shard_map/all_to_all | solution.py:45
  33.2 3.6 all-to-all-start
  37.0 1.6 copy.66
  38.6 24.2 %all-to-all-done = f32[1,8,1,8,4096]{4,3,2,0,1:T(8,128)S(1)} async-done(((f32[1,8,1,8,4096]{4,3,2,0,1:T(8,128)}), f32[1,8,1,8,4096]{4,3,2,0,1:T(8,128)S(1)}, u32[]{:S(2)}, u32[]{:S(2)}) %all-to-all-start) | async-done | bytes 1048608 | tf_op jit(solution)/shard_map/all_to_all | solution.py:35
  62.7 3.5 all-to-all-start.4
  66.3 8.8 %copy.57 = f32[8,1,1,8,4096]{3,0,2,1,4:T(8,128)} copy(f32[8,1,1,8,4096]{4,3,0,2,1:T(8,128)S(1)} %bitcast.162) | data formatting | bytes 2097152 | tf_op jit(solution)/shard_map/all_to_all | solution.py:35
  75.1 11.9 %reshape.289 = f32[4,1,65536]{2,1,0:T(1,128)} reshape(f32[4096,1,1,8,8]{4,3,2,1,0:T(8,128)} %bitcast.145) | data formatting | bytes 2097152
  87.0 4.4 all-to-all-start.1
  91.5 1.9 fusion.62
  93.4 3.2 fusion.68
  96.7 9.1 %all-to-all-done.1 = f32[4,1,65536]{2,1,0:T(1,128)} async-done(((f32[4,1,65536]{2,1,0:T(1,128)}), f32[4,1,65536]{2,1,0:T(1,128)}, u32[]{:S(2)}, u32[]{:S(2)}) %all-to-all-start.1) | async-done | bytes 1048608 | tf_op jit(solution)/shard_map/all_to_all | solution.py:34
  105.7 0.5 broadcast.507
  106.2 4.5 reduce
  110.8 15.0 %reshape.290 = f32[4096,1,1,8,8]{4,3,2,1,0:T(8,128)} reshape(f32[4,65536]{1,0:T(4,128)S(1)} %reduce) | data formatting | bytes 2097152
  125.8 9.8 %copy.92 = f32[8,1,1,8,4,1024]{5,4,3,0,2,1:T(4,128)S(1)} copy(f32[8,1,1,8,4,1024]{3,0,5,4,2,1:T(8,128)} %bitcast.146) | data formatting | bytes 2097152 | tf_op jit(solution)/shard_map/all_to_all | solution.py:34
  135.6 0.6 copy.59
  136.3 1.9 fusion.64
  138.2 4.8 subtract_bitcast_fusion.1
  143.0 0.6 pad_maximum_fusion.1
  143.6 4.4 copy.67
  148.0 4.7 all-to-all-start.5
  152.7 2.0 pad_maximum_fusion
  154.7 4.5 copy.60
  159.2 86.8 %all-to-all-done.5 = f32[2,16,32,1024]{3,2,0,1:T(8,128)} async-done(((f32[2,16,32,1024]{3,2,0,1:T(8,128)}), f32[2,16,32,1024]{3,2,0,1:T(8,128)}, u32[]{:S(2)}, u32[]{:S(2)}) %all-to-all-start.5) | async-done | bytes 4194336 | tf_op jit(solution)/shard_map/all_to_all | solution.py:113
  246.0 5.0 all-to-all-start.2
  251.2 2.5 copy.68
  253.7 0.6 fusion.169
  254.3 0.2 copy.69
  254.6 0.2 copy.71
  254.8 4.4 fusion.31
  259.2 5.8 %fusion.27 = f32[2,1024,256]{2,1,0:T(8,128)} fusion(f32[2,256,1024]{2,1,0:T(8,128)S(1)} %bitcast.149, s32[256]{0:T(256)S(1)} %fusion.88), kind=kOutput, calls=%fused_computation.50 | convolution fusion | flops 1611530240 | bytes 4195328 | tf_op jit(solution)/shard_map/qp,jpc->jqc/dot_general | solution.py:15
  265.0 6.0 %convolution_add_fusion = f32[2,1024,256]{2,1,0:T(8,128)} fusion(f32[2,1024,256]{2,1,0:T(8,128)S(1)} %fusion.31, f32[2,256,1024]{2,1,0:T(8,128)S(1)} %bitcast.150, s32[256]{0:T(256)S(1)} %fusion.88), kind=kOutput, calls=%fused_computation.23 | convolution fusion | flops 1612054528 | bytes 6292480 | tf_op jit(solution)/shard_map/qp,jpc->jqc/dot_general | solution.py:15
  271.1 72.0 %all-to-all-done.2 = f32[2,16,32,1024]{3,2,0,1:T(8,128)} async-done(((f32[2,16,32,1024]{3,2,0,1:T(8,128)}), f32[2,16,32,1024]{3,2,0,1:T(8,128)}, u32[]{:S(2)}, u32[]{:S(2)}) %all-to-all-start.2) | async-done | bytes 4194336 | tf_op jit(solution)/shard_map/all_to_all | solution.py:110
  343.1 2.5 copy.61
  345.6 0.6 fusion.170
  346.4 4.4 fusion.33
  351.1 4.5 fusion.29
  355.6 4.7 convolution_add_fusion.1
  360.3 4.3 convolution_subtract_fusion
  364.7 5.0 multiply_subtract_fusion
  369.7 2.8 fusion.2
  372.5 2.8 fusion
  375.3 2.9 fusion.8
  378.3 3.3 subtract_bitcast_fusion
  381.6 2.2 pad_maximum_fusion.2
  383.8 7.4 %copy.77 = f32[2,2,256,1024]{3,1,0,2:T(2,128)} copy(f32[2,2,256,1024]{2,3,1,0:T(8,128)} %pad_maximum_fusion.2) | data formatting | bytes 8388608 | tf_op jit(solution)/shard_map/stack | solution.py:135
  391.3 96.9 %all_to_all.116 = f32[2,2,256,1024]{3,1,0,2:T(2,128)S(1)} all-to-all(f32[2,2,256,1024]{3,1,0,2:T(2,128)} %copy.77), channel_id=1, replica_groups=mesh['seq'=8,'ch'=4] {'seq'}, dimensions={2} | all-to-all | bytes 8388608 | tf_op jit(solution)/shard_map/all_to_all | solution.py:134
  488.2 2.4 copy.78
  490.6 1.8 fusion.168
  492.4 1.6 copy.79
  494.1 2.4 squeeze.22
  496.5 2.9 fusion.66
  499.4 3.0 copy.80
  502.3 2.7 squeeze.23
  505.0 1.1 fusion.14
  506.2 0.6 copy.81
  506.8 28.9 %all_to_all.117 = f32[8,1,4,8,1024]{4,3,2,1,0:T(8,128)S(1)} all-to-all(f32[8,1,4,8,1024]{4,3,2,1,0:T(8,128)S(1)} %copy.81), channel_id=1, replica_groups=mesh['seq'=8,'ch'=4] {'seq'}, dimensions={0} | all-to-all | bytes 2097152 | tf_op jit(solution)/shard_map/all_to_all | solution.py:142
  535.7 0.6 copy.82
  536.3 16.9 %all_to_all.118 = f32[1,8,4,8,1024]{4,1,3,0,2:T(8,128)S(1)} all-to-all(f32[1,8,4,8,1024]{4,1,3,0,2:T(8,128)S(1)} %copy.82), channel_id=1, replica_groups=mesh['seq'=8,'ch'=4] {'ch'}, dimensions={2} | all-to-all | bytes 2097152 | tf_op jit(solution)/shard_map/all_to_all | solution.py:141
  553.2 0.7 copy.95
  553.9 0.6 copy.93
  554.6 1.1 multiply_convert_fusion
  (33 shorter events, 1.1 us)
Async XLA Ops:
  0.0 7.4 %copy-start.7 = (bf16[64,4096]{1,0:T(8,128)(2,1)S(1)}, bf16[64,4096]{1,0:T(8,128)(2,1)}, u32[]{:S(2)}) copy-start(bf16[64,4096]{1,0:T(8,128)(2,1)} %param.6) | copy-start | bytes 1572868
  0.0 7.4 %copy-start.5 = (bf16[64,4096]{1,0:T(8,128)(2,1)S(1)}, bf16[64,4096]{1,0:T(8,128)(2,1)}, u32[]{:S(2)}) copy-start(bf16[64,4096]{1,0:T(8,128)(2,1)} %param.7) | copy-start | bytes 1572868
  0.0 33.2 %all-to-all-start.3 = ((f32[1,8,1,8,4096]{4,3,2,0,1:T(8,128)}), f32[1,8,1,8,4096]{4,3,2,0,1:T(8,128)S(1)}, u32[]{:S(2)}, u32[]{:S(2)}) async-start(f32[1,8,1,8,4096]{4,3,2,0,1:T(8,128)} %bitcast.170), calls=%async_computation.3 | async-start | bytes 2097152 | tf_op jit(solution)/shard_map/all_to_all | solution.py:45
  33.2 29.5 %all-to-all-start = ((f32[1,8,1,8,4096]{4,3,2,0,1:T(8,128)}), f32[1,8,1,8,4096]{4,3,2,0,1:T(8,128)S(1)}, u32[]{:S(2)}, u32[]{:S(2)}) async-start(f32[1,8,1,8,4096]{4,3,2,0,1:T(8,128)} %fusion.15), calls=%async_computation | async-start | bytes 2097152 | tf_op jit(solution)/shard_map/all_to_all | solution.py:35
  62.7 24.2 %all-to-all-start.4 = ((f32[4,8,1,1,8,1024]{5,1,4,3,2,0:T(8,128)}), f32[4,8,1,1,8,1024]{5,1,4,3,2,0:T(8,128)S(1)}, u32[]{:S(2)}, u32[]{:S(2)}) async-start(f32[4,8,1,1,8,1024]{5,1,4,3,2,0:T(8,128)} %copy.66), calls=%async_computation.4 | async-start | bytes 2097152 | tf_op jit(solution)/shard_map/all_to_all | solution.py:42
  87.0 18.8 %all-to-all-start.1 = ((f32[4,1,65536]{2,1,0:T(1,128)}), f32[4,1,65536]{2,1,0:T(1,128)}, u32[]{:S(2)}, u32[]{:S(2)}) async-start(f32[4,1,65536]{2,1,0:T(1,128)} %reshape.289), calls=%async_computation.1 | async-start | bytes 2097152 | tf_op jit(solution)/shard_map/all_to_all | solution.py:34
  136.2 1.9 copy-start
  148.0 4.7 copy-start.2
  148.0 98.0 %all-to-all-start.5 = ((f32[2,16,32,1024]{3,2,0,1:T(8,128)}), f32[2,16,32,1024]{3,2,0,1:T(8,128)}, u32[]{:S(2)}, u32[]{:S(2)}) async-start(f32[2,16,32,1024]{3,2,0,1:T(8,128)} %copy.67), calls=%async_computation.5 | async-start | bytes 8388608 | tf_op jit(solution)/shard_map/all_to_all | solution.py:113
  246.0 97.1 %all-to-all-start.2 = ((f32[2,16,32,1024]{3,2,0,1:T(8,128)}), f32[2,16,32,1024]{3,2,0,1:T(8,128)}, u32[]{:S(2)}, u32[]{:S(2)}) async-start(f32[2,16,32,1024]{3,2,0,1:T(8,128)} %copy.60), calls=%async_computation.2 | async-start | bytes 8388608 | tf_op jit(solution)/shard_map/all_to_all | solution.py:110
  355.5 4.7 copy-start.1
  360.3 4.3 copy-start.4
  496.5 2.9 copy-start.3
  553.2 1.3 copy-start.6
  553.2 1.3 copy-start.8
  553.2 1.4 copy-start.9
  553.2 1.4 copy-start.10
